TPU v7x, 32 devices: a whole 2x2x4 slice. The times are simulated.
32 devices in a mesh: grp: 2 (over y), row: 8 (over z, x), head: 2 (over core).
Axes of the slice: x: 2, y: 2, z: 4, core: 2. Of those that a mesh axis runs over, the one named last changes fastest.
Arguments:
- latent: bfloat16 [16, 256, 512], P(('grp', 'row')), parts along dimension 0, may hold values from -6 to 6
- weights: bfloat16 [512, 8, 512], P(None, None, 'head'), may hold values from -0.25 to 0.25
- cotangent: bfloat16 [16, 256, 512], P(('grp', 'row')), parts along dimension 0, may hold values from -6 to 6
Outputs:
- latent_grad: bfloat16 [16, 256, 512], P(('grp', 'row')), parts along dimension 0
- weight_grad: float32 [1024, 8, 512], P(('grp', 'row'), None, 'head'), parts along dimension 0
There are 2 independent parts, one for each index of `grp`. A program takes and returns all parts, laid end to end along the dimension named above; an argument that names none is the same for every part. Nothing has to cross between parts.
All inputs are finite; a program needn't handle non-finite values.
Results may differ from a plain program's by a relative error of at most 0.03.
Values may be sent and summed in bfloat16 or wider, within the bound.
A program may use at most 64 MiB of HBM per device.

v0:
```python
import math
import jax
import jax.numpy as jnp
from jax import lax
from jax.sharding import PartitionSpec as P

HEAD_DIM = 64
epsilon = 1e-06


def index_pair(pattern):
    return (pattern + "hd", pattern.replace("l", "m") + "hd")


def head_norm(values):
    inverse = lax.rsqrt(jnp.mean(values * values, axis=-1, keepdims=True) + epsilon)
    return (values * inverse, inverse)


def three_maps(weights, first):
    width = weights.shape[0]
    return weights[:, first : first + 3, :].reshape(width, 3 * weights.shape[2])


def attend_local(inputs, weights, first, pattern):
    outer, inner, width = inputs.shape
    local = weights.shape[2]
    heads_here = local // HEAD_DIM
    logit_scale = 2.0 / math.sqrt(HEAD_DIM)
    flat = inputs.reshape(outer * inner, width)
    joined = jnp.dot(flat, three_maps(weights, first), preferred_element_type=jnp.float32)
    shaped = joined.reshape(outer, inner, 3, heads_here, HEAD_DIM)
    query_n, query_r = head_norm(shaped[:, :, 0])
    key_n, key_r = head_norm(shaped[:, :, 1])
    query_batched = query_n.astype(jnp.bfloat16)
    key_batched = key_n.astype(jnp.bfloat16)
    value_batched = shaped[:, :, 2].astype(jnp.bfloat16)
    query_ix, key_ix = index_pair(pattern)
    attention_logits = logit_scale * jnp.einsum(
        query_ix + "," + key_ix + "->shlm",
        query_batched,
        key_batched,
        preferred_element_type=jnp.float32,
    )
    expo = jnp.exp(attention_logits)
    probs = expo / jnp.sum(expo, axis=-1, keepdims=True)
    probability_batched = probs.astype(jnp.bfloat16)
    attention_output = jnp.einsum(
        "shlm," + key_ix + "->" + query_ix,
        probability_batched,
        value_batched,
        preferred_element_type=jnp.float32,
    ).astype(jnp.bfloat16)
    saved = (
        query_n,
        query_r,
        query_batched,
        key_n,
        key_r,
        key_batched,
        value_batched,
        probs,
        probability_batched,
    )
    return (flat, saved, attention_output.reshape(outer * inner, local))


def attend_back(saved, upstream, weights, first, pattern):
    outer, inner, width = upstream.shape
    local = weights.shape[2]
    heads_here = local // HEAD_DIM
    logit_scale = 2.0 / math.sqrt(HEAD_DIM)
    (
        query_n,
        query_r,
        query_batched,
        key_n,
        key_r,
        key_batched,
        value_batched,
        probs,
        probability_batched,
    ) = saved
    query_ix, key_ix = index_pair(pattern)
    grad_flat = upstream.reshape(outer * inner, width)
    grad_att = jnp.dot(
        grad_flat, weights[:, first + 3, :], preferred_element_type=jnp.float32
    ).astype(jnp.bfloat16)
    grad_att = grad_att.reshape(outer, inner, heads_here, HEAD_DIM)
    gradient_value_rows = jnp.einsum(
        "shlm," + query_ix + "->" + key_ix,
        probability_batched,
        grad_att,
        preferred_element_type=jnp.float32,
    ).astype(jnp.bfloat16)
    gradient_probability = jnp.einsum(
        query_ix + "," + key_ix + "->shlm",
        grad_att,
        value_batched,
        preferred_element_type=jnp.float32,
    )
    delta = jnp.sum(probs * gradient_probability, axis=-1, keepdims=True)
    gradient_logits = (probs * (gradient_probability - delta)).astype(jnp.bfloat16)
    gradient_normed_query = logit_scale * jnp.einsum(
        "shlm," + key_ix + "->" + query_ix,
        gradient_logits,
        key_batched,
        preferred_element_type=jnp.float32,
    )
    gradient_normed_key = logit_scale * jnp.einsum(
        "shlm," + query_ix + "->" + key_ix,
        gradient_logits,
        query_batched,
        preferred_element_type=jnp.float32,
    )
    grad_query = (
        query_r
        * (
            gradient_normed_query
            - query_n * jnp.mean(gradient_normed_query * query_n, axis=-1, keepdims=True)
        )
    ).astype(jnp.bfloat16)
    grad_key = (
        key_r
        * (
            gradient_normed_key
            - key_n * jnp.mean(gradient_normed_key * key_n, axis=-1, keepdims=True)
        )
    ).astype(jnp.bfloat16)
    stacked = jnp.stack([grad_query, grad_key, gradient_value_rows], axis=2).reshape(
        outer * inner, 3 * local
    )
    partial_in = lax.dot_general(
        stacked,
        three_maps(weights, first),
        (((1,), (1,)), ((), ())),
        preferred_element_type=jnp.float32,
    )
    return (partial_in, stacked, grad_flat)


def weight_terms(flat, stacked, grad_flat, attention_output, count):
    contract = (((0,), (0,)), ((), ()))
    three = lax.dot_general(flat, stacked, contract, preferred_element_type=jnp.float32)
    last = lax.dot_general(
        grad_flat, attention_output, contract, preferred_element_type=jnp.float32
    )
    return jnp.concatenate((three.reshape(count, 3, -1), last.reshape(count, 1, -1)), 1)


def head_sum(partial_value):
    return lax.psum(partial_value.astype(jnp.bfloat16), "head").astype(jnp.float32)


def on_device(latent, weights, cotangent):
    rows, cols, width = latent.shape
    rows_here = width // lax.axis_size("row")
    flat_row, saved_row, attended_row = attend_local(latent, weights, 0, "sl")
    mixed = head_sum(
        lax.dot_general(
            attended_row,
            weights[:, 3, :],
            (((1,), (1,)), ((), ())),
            preferred_element_type=jnp.float32,
        )
    )
    first_out = (latent.astype(jnp.float32) + mixed.reshape(rows, cols, width)).astype(jnp.bfloat16)
    columns, cotangent_cols = (
        lax.all_to_all(first_out, "row", split_axis=1, concat_axis=0, tiled=True),
        lax.all_to_all(cotangent, "row", split_axis=1, concat_axis=0, tiled=True),
    )
    height = columns.shape[0]
    flat_col, saved_col, attended_col = attend_local(columns, weights, 4, "ls")
    partial_col, stacked_col, grad_col = attend_back(saved_col, cotangent_cols, weights, 4, "ls")
    grad_mid = (
        cotangent_cols.astype(jnp.float32) + head_sum(partial_col).reshape(columns.shape)
    ).astype(jnp.bfloat16)
    grad_first = lax.all_to_all(grad_mid, "row", split_axis=0, concat_axis=1, tiled=True)
    partial_row, stacked_row, grad_row = attend_back(saved_row, grad_first, weights, 0, "sl")
    latent_grad = (
        grad_first.astype(jnp.float32) + head_sum(partial_row).reshape(latent.shape)
    ).astype(jnp.bfloat16)
    summed = lax.psum_scatter(
        jnp.concatenate(
            (
                weight_terms(
                    flat_row, stacked_row, grad_row, attended_row, rows_here * lax.axis_size("row")
                ),
                weight_terms(
                    flat_col, stacked_col, grad_col, attended_col, rows_here * lax.axis_size("row")
                ),
            ),
            1,
        ),
        "row",
        scatter_dimension=0,
        tiled=True,
    )
    weight_grad = summed * (1.0 / math.sqrt(height * cols))
    return (latent_grad, weight_grad)


def solution(mesh):
    in_specs = (P(("grp", "row"), None, None), P(None, None, "head"), P(("grp", "row"), None, None))
    out_specs = (P(("grp", "row"), None, None), P(("grp", "row"), None, "head"))
    return jax.shard_map(
        on_device, mesh=mesh, in_specs=in_specs, out_specs=out_specs, check_vma=False
    )
```

profile of v0, /device:TPU:0, one launch (start us, length us, event | category | flops | bytes accessed | tf_op | source)
XLA Modules:
  0.0 247.7 jit_solution(1502684918247256493)
XLA Ops:
  7.2 4.4 %fusion.70 = (bf16[512,1,256]{2,1,0:T(2,128)(2,1)}, bf16[512,1,256]{2,1,0:T(2,128)(2,1)}) fusion(bf16[512,8,256]{2,1,0:T(8,128)(2,1)} %param.4), kind=kLoop, calls=%fused_computation.123 | loop fusion | bytes 1048576 | tf_op jit(solution)/shard_map/slice | solution.py:162
  15.9 1.0 fusion.2
  16.9 2.1 copy.187
  19.6 3.0 %reduce.8 = bf16[256,512]{1,0:T(8,128)(2,1)S(1)} reduce(bf16[256,1,512]{2,1,0:T(2,128)(2,1)} %bitcast.232, bf16[]{:T(256)} %broadcast.179), dimensions={1}, to_apply=%bitcast.221.reduce_sub_computation | reduce | bytes 524290
  23.5 7.3 %all-to-all-start = ((bf16[8,2,8192]{2,1,0:T(2,128)(2,1)}), bf16[8,2,8192]{2,1,0:T(2,128)(2,1)}, u32[]{:S(2)}, u32[]{:S(2)}) async-start(bf16[8,2,8192]{2,1,0:T(2,128)(2,1)} %reshape.315), calls=%async_computation | async-start | bytes 524288 | tf_op jit(solution)/shard_map/all_to_all | solution.py:170
  30.7 7.3 %all-reduce.4.cloned.1.call-done = bf16[1,256,512]{2,1,0:T(8,128)(2,1)} async-done(((bf16[1,256,512]{2,1,0:T(8,128)(2,1)}), bf16[1,256,512]{2,1,0:T(8,128)(2,1)}) %all-reduce.4.cloned.1.call-update) | async-done | bytes 262160 | tf_op jit(solution)/shard_map/psum | solution.py:152
  38.0 1.0 add_convert_fusion.1
  39.4 2.8 %reduce.9 = bf16[256,512]{1,0:T(8,128)(2,1)} reduce(bf16[256,1,512]{2,1,0:T(2,128)(2,1)S(1)} %bitcast.233, bf16[]{:T(256)} %broadcast.179), dimensions={1}, to_apply=%bitcast.220.reduce_sub_computation | reduce | bytes 524290
  42.3 1.8 reshape.317
  44.1 5.8 %all-to-all-start.1 = ((bf16[8,2,8192]{2,1,0:T(2,128)(2,1)}), bf16[8,2,8192]{2,1,0:T(2,128)(2,1)}, u32[]{:S(2)}, u32[]{:S(2)}) async-start(bf16[8,2,8192]{2,1,0:T(2,128)(2,1)} %reshape.317), calls=%async_computation.1 | async-start | bytes 524288 | tf_op jit(solution)/shard_map/all_to_all | solution.py:169
  50.1 1.6 copy.134
  51.8 1.2 reshape.316
  54.8 4.5 %all-to-all-done.1 = bf16[8,2,8192]{2,1,0:T(2,128)(2,1)} async-done(((bf16[8,2,8192]{2,1,0:T(2,128)(2,1)}), bf16[8,2,8192]{2,1,0:T(2,128)(2,1)}, u32[]{:S(2)}, u32[]{:S(2)}) %all-to-all-start.1) | async-done | bytes 262176 | tf_op jit(solution)/shard_map/all_to_all | solution.py:169
  59.4 1.2 reshape.318
  61.4 1.8 fusion.75
  64.2 1.2 fusion.44
  66.6 1.2 fusion.1
  67.8 3.3 %multiply_reduce_fusion.1 = (f32[32,4,8]{2,1,0:T(4,128)}, f32[32,4,8,8]{2,3,1,0:T(8,128)}) fusion(f32[32,4,8,8]{2,3,1,0:T(8,128)} %fusion.44, bf16[8,32,4,64]{3,1,2,0:T(8,128)(2,1)} %copy-done.12, bf16[8,32,4,64]{3,1,2,0:T(8,128)(2,1)} %copy-done.14), kind=kOutput, calls=%fused_computation.46 | convolution fusion | flops 1081351 | bytes 331776 | tf_op jit(solution)/shard_map/div | solution.py:46
  71.1 1.4 multiply_convert_fusion.1
  72.4 2.0 fusion.49
  74.5 1.1 fusion.41
  75.6 2.4 fusion.46
  78.0 1.1 copy.185
  79.2 2.1 fusion.11
  81.4 1.0 fusion.22
  82.6 1.3 copy.109
  83.9 1.9 reshape.297
  85.9 1.1 convolution_convert_fusion.2
  87.0 17.4 %all-reduce.6.cloned.1.call-done = bf16[8,32,512]{2,1,0:T(8,128)(2,1)} async-done(((bf16[8,32,512]{2,1,0:T(8,128)(2,1)}), bf16[8,32,512]{2,1,0:T(8,128)(2,1)}) %all-reduce.6.cloned.1.call-update) | async-done | bytes 262160 | tf_op jit(solution)/shard_map/psum | solution.py:152
  104.4 1.7 fusion.7
  106.1 5.9 %all-to-all-start.2 = ((bf16[8,32,512]{2,1,0:T(8,128)(2,1)}), bf16[8,32,512]{2,1,0:T(8,128)(2,1)}, u32[]{:S(2)}, u32[]{:S(2)}) async-start(bf16[8,32,512]{2,1,0:T(8,128)(2,1)} %fusion.7), calls=%async_computation.2 | async-start | bytes 524288 | tf_op jit(solution)/shard_map/all_to_all | solution.py:178
  112.0 2.4 fusion.3
  114.4 1.1 copy.113
  115.5 1.1 copy.117
  116.8 0.9 copy.114
  117.7 1.1 convolution_bitcast_fusion.1
  118.8 1.5 fusion.28
  120.3 1.2 all-to-all-done.2
  121.5 1.4 convolution_convert_fusion.5
  126.3 1.1 convolution_convert_fusion.1
  127.4 2.0 convolution_bitcast_fusion.2
  129.5 1.7 copy.119
  131.1 4.1 %pad_maximum_fusion = f32[512,8,256]{2,0,1:T(8,128)} fusion(f32[512,1,256]{2,0,1:T(8,128)} %convolution_bitcast_fusion.1, f32[512,3,256]{2,0,1:T(8,128)S(1)} %fusion.28, f32[512,1,256]{2,0,1:T(8,128)} %convolution_bitcast_fusion.2, f32[512,3,256]{2,0,1:T(8,128)} %copy.119), kind=kLoop, calls=%fused_computation | loop fusion | flops 3145728 | bytes 8388608 | tf_op jit(solution)/shard_map/concatenate | solution.py:184
  135.2 10.7 %all-reduce.8.cloned.1.call-done = bf16[256,512]{1,0:T(8,128)(2,1)} async-done(((bf16[256,512]{1,0:T(8,128)(2,1)}), bf16[256,512]{1,0:T(8,128)(2,1)}) %all-reduce.8.cloned.1.call-update) | async-done | bytes 262160 | tf_op jit(solution)/shard_map/psum | solution.py:152
  145.9 1.8 fusion.20
  147.7 91.2 %reduce-scatter.2.cloned.1.call-done = f32[64,8,256]{2,0,1:T(8,128)} async-done(((f32[512,8,256]{2,0,1:T(8,128)}), f32[64,8,256]{2,0,1:T(8,128)}) %reduce-scatter.2.cloned.1.call-update) | async-done | bytes 524304 | tf_op jit(solution)/shard_map/reduce_scatter | solution.py:183
  239.0 1.1 broadcast_multiply_fusion
  240.1 1.1 copy.120
  (103 shorter events, 14.9 us)
Async XLA Ops:
  7.2 30.8 %all-reduce.4.cloned.1.call-start = ((), (), s32[]{:S(2)}) async-start(), calls=%async_computation.4 | async-start | bytes 524288 | tf_op jit(solution)/shard_map/psum | solution.py:152
  7.2 4.4 %copy-start.3 = (bf16[512,8,256]{2,1,0:T(8,128)(2,1)S(1)}, bf16[512,8,256]{2,1,0:T(8,128)(2,1)}, u32[]{:S(2)}) copy-start(bf16[512,8,256]{2,1,0:T(8,128)(2,1)} %param.4) | copy-start | bytes 6291460
  12.3 1.0 copy-start.10
  13.2 0.9 copy-start.8
  13.8 0.6 copy-start.26
  13.8 0.6 copy-start.28
  14.1 0.7 copy-start.20
  14.1 0.7 copy-start.22
  14.8 1.0 copy-start.15
  23.5 20.6 %all-to-all-start = ((bf16[8,2,8192]{2,1,0:T(2,128)(2,1)}), bf16[8,2,8192]{2,1,0:T(2,128)(2,1)}, u32[]{:S(2)}, u32[]{:S(2)}) async-start(bf16[8,2,8192]{2,1,0:T(2,128)(2,1)} %reshape.315), calls=%async_computation | async-start | bytes 524288 | tf_op jit(solution)/shard_map/all_to_all | solution.py:170
  44.1 15.3 %all-to-all-start.1 = ((bf16[8,2,8192]{2,1,0:T(2,128)(2,1)}), bf16[8,2,8192]{2,1,0:T(2,128)(2,1)}, u32[]{:S(2)}, u32[]{:S(2)}) async-start(bf16[8,2,8192]{2,1,0:T(2,128)(2,1)} %reshape.317), calls=%async_computation.1 | async-start | bytes 524288 | tf_op jit(solution)/shard_map/all_to_all | solution.py:169
  49.9 54.5 %all-reduce.6.cloned.1.call-start = ((), (), s32[]{:S(2)}) async-start(), calls=%async_computation.5 | async-start | bytes 524288 | tf_op jit(solution)/shard_map/psum | solution.py:152
  50.1 3.6 %copy-start.16 = (bf16[512,1,256]{2,1,0:T(2,128)(2,1)S(1)}, bf16[512,1,256]{2,1,0:T(2,128)(2,1)}, u32[]{:S(2)}) copy-start(bf16[512,1,256]{2,1,0:T(2,128)(2,1)} %get-tuple-element.21) | copy-start | bytes 786436
  53.0 0.7 copy-start.6
  60.6 0.8 copy-start.1
  61.4 2.9 %copy-start.19 = (bf16[8,32,4,64]{3,2,1,0:T(4,128)(2,1)S(1)}, bf16[8,32,4,64]{3,2,1,0:T(4,128)(2,1)}, u32[]{:S(2)}) copy-start(bf16[8,32,4,64]{3,2,1,0:T(4,128)(2,1)} %reshape.296) | copy-start | bytes 393220
  63.5 0.7 copy-start.17
  64.2 1.2 copy-start.24
  65.8 0.7 copy-start.12
  65.8 0.8 copy-start.14
  71.1 3.4 %copy-start.13 = (bf16[8,32,4,64]{3,1,2,0:T(8,128)(2,1)S(1)}, bf16[8,32,4,64]{3,1,2,0:T(8,128)(2,1)}, u32[]{:S(2)}) copy-start(bf16[8,32,4,64]{3,1,2,0:T(8,128)(2,1)} %copy-done.12) | copy-start | bytes 393220
  78.0 3.3 %copy-start.4 = (f32[32,4,64,8]{2,3,1,0:T(8,128)S(1)}, f32[32,4,64,8]{2,3,1,0:T(8,128)}, u32[]{:S(2)}) copy-start(f32[32,4,64,8]{2,3,1,0:T(8,128)} %fusion.49) | copy-start | bytes 786436
  78.0 3.3 %copy-start.5 = (f32[32,4,64,8]{2,3,1,0:T(8,128)S(1)}, f32[32,4,64,8]{2,3,1,0:T(8,128)}, u32[]{:S(2)}) copy-start(f32[32,4,64,8]{2,3,1,0:T(8,128)} %fusion.41) | copy-start | bytes 786436
  78.0 3.3 %copy-start.25 = (f32[8,32,4]{1,2,0:T(4,128)S(1)}, f32[8,32,4]{1,2,0:T(4,128)}, u32[]{:S(2)}) copy-start(f32[8,32,4]{1,2,0:T(4,128)} %copy-done.24) | copy-start | bytes 12292
  82.6 3.3 %copy-start = (bf16[512,3,256]{0,2,1:T(8,128)(2,1)S(1)}, bf16[512,3,256]{0,2,1:T(8,128)(2,1)}, u32[]{:S(2)}) copy-start(bf16[512,3,256]{0,2,1:T(8,128)(2,1)} %copy.134) | copy-start | bytes 2359300
  83.9 20.5 %copy-start.7 = (bf16[1,256,512]{2,1,0:T(8,128)(2,1)S(1)}, bf16[1,256,512]{2,1,0:T(8,128)(2,1)}, u32[]{:S(2)}) copy-start(bf16[1,256,512]{2,1,0:T(8,128)(2,1)} %copy-done.6) | copy-start | bytes 786436
  86.9 25.1 %copy-start.18 = (bf16[8,32,4,64]{3,1,2,0:T(8,128)(2,1)S(1)}, bf16[8,32,4,64]{3,1,2,0:T(8,128)(2,1)}, u32[]{:S(2)}) copy-start(bf16[8,32,4,64]{3,1,2,0:T(8,128)(2,1)} %copy-done.17) | copy-start | bytes 393220
  106.1 8.3 %copy-start.2 = (bf16[256,1,512]{2,1,0:T(2,128)(2,1)S(1)}, bf16[256,1,512]{2,1,0:T(2,128)(2,1)}, u32[]{:S(2)}) copy-start(bf16[256,1,512]{2,1,0:T(2,128)(2,1)} %copy-done.1) | copy-start | bytes 786436
  106.1 15.4 %all-to-all-start.2 = ((bf16[8,32,512]{2,1,0:T(8,128)(2,1)}), bf16[8,32,512]{2,1,0:T(8,128)(2,1)}, u32[]{:S(2)}, u32[]{:S(2)}) async-start(bf16[8,32,512]{2,1,0:T(8,128)(2,1)} %fusion.7), calls=%async_computation.2 | async-start | bytes 524288 | tf_op jit(solution)/shard_map/all_to_all | solution.py:178
  112.0 34.0 %all-reduce.8.cloned.1.call-start = ((), (), s32[]{:S(2)}) async-start(), calls=%async_computation.6 | async-start | bytes 524288 | tf_op jit(solution)/shard_map/psum | solution.py:152
  123.5 0.9 copy-start.23
  123.5 1.2 copy-start.21
  123.5 1.2 copy-start.27
  123.6 1.2 copy-start.29
  124.7 1.0 copy-start.11
  125.1 1.2 copy-start.9
  127.4 111.6 %reduce-scatter.2.cloned.1.call-start = ((), (), s32[]{:S(2)}) async-start(), calls=%async_computation.7 | async-start | bytes 4718592 | tf_op jit(solution)/shard_map/reduce_scatter | solution.py:183
Sparse Core Ops, SparseCore 0:
  17.0 20.9 all-reduce.3
  87.1 17.2 all-reduce.5
  127.5 18.3 all-reduce.7
  149.9 89.0 reduce-scatter.1
where the time goes:
time: 249 us; the launch traced here: 248 us
  waiting for transfers between devices  132 us (53%)
  local copies, waits for them, and re-layouts  33 us (13%)
  matrix products  27.3 us (11%)
  other arithmetic  21.5 us (9%)
  starting transfers between devices  19.3 us (8%)
  between operations  14.3 us (6%)
    reduce_scatter x1, waiting for transfers between devices, on_device(): lax.psum_scatter(jnp.concatenate((weight_terms(flat_row, stacked_row, gra...  91.2 us
    psum x3, waiting for transfers between devices, head_sum(): lax.psum(partial_value.astype(jnp.bfloat16), 'head').astype(jnp.float32)  35.4 us
    unnamed x70, local copies, waits for them, and re-layouts  17.2 us
    all_to_all x1, starting transfers between devices, on_device(): lax.all_to_all(cotangent, 'row', split_axis=1, concat_axis=0, tiled=True)  7.26 us
    all_to_all x1, starting transfers between devices, on_device(): lax.all_to_all(grad_mid, 'row', split_axis=0, concat_axis=1, tiled=True)  5.9 us
    unnamed x2, other arithmetic  5.87 us
    all_to_all x1, starting transfers between devices, on_device(): lax.all_to_all(first_out, 'row', split_axis=1, concat_axis=0, tiled=True)  5.77 us
  transfers between devices with their start and end apart: 7, of which 6 were waited for; matrix products, arithmetic and copies ran while one was open for 14% of the time, Pallas kernels for 0%

commit v1 on v0

--- a/solution.py
+++ b/solution.py
@@ -149,7 +149,9 @@
 
 
 def head_sum(partial_value):
-    return lax.psum(partial_value.astype(jnp.bfloat16), "head").astype(jnp.float32)
+    return jnp.sum(lax.all_gather(partial_value.astype(jnp.bfloat16), "head"), axis=0).astype(
+        jnp.float32
+    )
 
 
 def on_device(latent, weights, cotangent):

time: 249 us -> 215 us (0.86)
  waiting for transfers between devices: 132 us -> 89 us
  blocking collectives: 0 us -> 6.76 us
  starting transfers between devices: 19.3 us -> 16 us
  local copies, waits for them, and re-layouts: 33 us -> 36.1 us
    psum x3 -> x0, waiting for transfers between devices: 35.4 us -> none  [head_sum(): lax.psum(partial_value.astype(jnp.bfloat16), 'head').astype(jnp.float32)]
    reduce_scatter x1, waiting for transfers between devices: 91.2 us -> 81.5 us  [on_device(): lax.psum_scatter(jnp.concatenate((weight_terms(flat_row, stacked_row, gra...]
    all_gather x0 -> x3, blocking collectives: none -> 6.76 us  [head_sum(): lax.all_gather(partial_value.astype(jnp.bfloat16), 'head')]
    all_to_all x1, waiting for transfers between devices: 0.01 us -> 3.32 us  [on_device(): lax.all_to_all(cotangent, 'row', split_axis=1, concat_axis=0, tiled=True)]
    all_to_all x1, waiting for transfers between devices: 4.54 us -> 1.59 us  [on_device(): lax.all_to_all(first_out, 'row', split_axis=1, concat_axis=0, tiled=True)]
    all_to_all x1, starting transfers between devices: 7.26 us -> 4.41 us  [on_device(): lax.all_to_all(cotangent, 'row', split_axis=1, concat_axis=0, tiled=True)]
    unnamed x70 -> x66, local copies, waits for them, and re-layouts: 17.2 us -> 18.5 us
  transfers between devices with their start and end apart: 7 -> 4, of which waited for: 6 -> 4; matrix products, arithmetic and copies ran while one was open for 14% -> 10% of each run, Pallas kernels for 0% -> 0%
where the time goes in v1:
time: 215 us; the launch traced here: 213 us
  waiting for transfers between devices  89 us (41%)
  local copies, waits for them, and re-layouts  36.1 us (17%)
  matrix products  28.3 us (13%)
  other arithmetic  22.2 us (10%)
  starting transfers between devices  16 us (7%)
  between operations  14.5 us (7%)
  blocking collectives  6.76 us (3%)
    reduce_scatter x1, waiting for transfers between devices, on_device(): lax.psum_scatter(jnp.concatenate((weight_terms(flat_row, stacked_row, gra...  81.5 us
    unnamed x66, local copies, waits for them, and re-layouts  18.5 us
    all_to_all x1, starting transfers between devices, on_device(): lax.all_to_all(first_out, 'row', split_axis=1, concat_axis=0, tiled=True)  7.18 us
    all_gather x3, blocking collectives, head_sum(): lax.all_gather(partial_value.astype(jnp.bfloat16), 'head')  6.76 us
    unnamed x2, other arithmetic  5.78 us
    slice x1, local copies, waits for them, and re-layouts, on_device(): weights[:, 3, :]  4.42 us
    all_to_all x1, starting transfers between devices, on_device(): lax.all_to_all(cotangent, 'row', split_axis=1, concat_axis=0, tiled=True)  4.41 us
  transfers between devices with their start and end apart: 4, of which 4 were waited for; matrix products, arithmetic and copies ran while one was open for 10% of the time, Pallas kernels for 0%

profile of v1, /device:TPU:0, one launch (start us, length us, event | category | flops | bytes accessed | tf_op | source)
XLA Modules:
  0.0 213.0 jit_solution(524430708681247044)
XLA Ops:
  7.2 4.4 %fusion.70 = (bf16[512,1,256]{2,1,0:T(2,128)(2,1)}, bf16[512,1,256]{2,1,0:T(2,128)(2,1)}) fusion(bf16[512,8,256]{2,1,0:T(8,128)(2,1)} %param.4), kind=kLoop, calls=%fused_computation.123 | loop fusion | bytes 1048576 | tf_op jit(solution)/shard_map/slice | solution.py:164
  16.1 2.4 %all-gather = bf16[512,512]{1,0:T(8,128)(2,1)} all-gather(bf16[256,512]{1,0:T(8,128)(2,1)S(1)} %convolution_convert_fusion.3), channel_id=2, replica_groups=mesh['grp'=2,'row'=8,'head'=2] {'head'}, dimensions={0}, use_global_device_ids=true | all-gather | bytes 786432 | tf_op jit(solution)/shard_map/all_gather | solution.py:152
  18.5 1.1 reduce_sum.147
  20.7 2.9 %reduce.12 = bf16[256,512]{1,0:T(8,128)(2,1)} reduce(bf16[256,1,512]{2,1,0:T(2,128)(2,1)S(1)} %bitcast.241, bf16[]{:T(256)} %broadcast.179), dimensions={1}, to_apply=%bitcast.228.reduce_sub_computation | reduce | bytes 524290
  23.6 1.9 reshape.350
  25.5 7.2 %all-to-all-start.1 = ((bf16[8,2,8192]{2,1,0:T(2,128)(2,1)}), bf16[8,2,8192]{2,1,0:T(2,128)(2,1)}, u32[]{:S(2)}, u32[]{:S(2)}) async-start(bf16[8,2,8192]{2,1,0:T(2,128)(2,1)} %reshape.350), calls=%async_computation.1 | async-start | bytes 524288 | tf_op jit(solution)/shard_map/all_to_all | solution.py:171
  32.6 1.4 copy.189
  34.0 2.9 %reduce.11 = bf16[256,512]{1,0:T(8,128)(2,1)} reduce(bf16[256,1,512]{2,1,0:T(2,128)(2,1)S(1)} %bitcast.244, bf16[]{:T(256)} %broadcast.179), dimensions={1}, to_apply=%bitcast.229.reduce_sub_computation | reduce | bytes 524290
  36.9 1.9 reshape.348
  38.8 1.6 copy.136
  40.4 1.6 all-to-all-done.1
  42.0 4.4 %all-to-all-start = ((bf16[8,2,8192]{2,1,0:T(2,128)(2,1)}), bf16[8,2,8192]{2,1,0:T(2,128)(2,1)}, u32[]{:S(2)}, u32[]{:S(2)}) async-start(bf16[8,2,8192]{2,1,0:T(2,128)(2,1)} %reshape.348), calls=%async_computation | async-start | bytes 524288 | tf_op jit(solution)/shard_map/all_to_all | solution.py:172
  46.4 1.2 reshape.351
  48.4 1.7 fusion.75
  51.8 3.3 %all-to-all-done = bf16[8,2,8192]{2,1,0:T(2,128)(2,1)} async-done(((bf16[8,2,8192]{2,1,0:T(2,128)(2,1)}), bf16[8,2,8192]{2,1,0:T(2,128)(2,1)}, u32[]{:S(2)}, u32[]{:S(2)}) %all-to-all-start) | async-done | bytes 262176 | tf_op jit(solution)/shard_map/all_to_all | solution.py:172
  55.1 1.9 reshape.349
  57.0 1.1 copy.92
  58.8 1.9 convolution_convert_fusion.6
  60.7 1.8 reshape.325
  64.0 2.2 %fusion.44 = f32[32,4,8,8]{2,3,1,0:T(8,128)} fusion(bf16[8,32,4,64]{3,1,2,0:T(8,128)(2,1)} %fusion.24, bf16[8,32,4,64]{3,2,1,0:T(4,128)(2,1)} %reshape.325), kind=kOutput, calls=%fused_computation.95 | convolution fusion | flops 1048576 | bytes 294912 | tf_op jit(solution)/shard_map/lshd,mshd->shlm/dot_general | solution.py:96
  67.4 1.2 fusion.1
  68.6 3.3 %multiply_reduce_fusion.1 = (f32[32,4,8]{2,1,0:T(4,128)}, f32[32,4,8,8]{2,3,1,0:T(8,128)}) fusion(f32[32,4,8,8]{2,3,1,0:T(8,128)} %fusion.44, bf16[8,32,4,64]{3,1,2,0:T(8,128)(2,1)} %copy-done.12, bf16[8,32,4,64]{3,1,2,0:T(8,128)(2,1)} %copy-done.14), kind=kOutput, calls=%fused_computation.48 | convolution fusion | flops 1081351 | bytes 331776 | tf_op jit(solution)/shard_map/div | solution.py:46
  71.8 1.4 multiply_convert_fusion.1
  73.2 2.0 fusion.49
  75.2 1.2 fusion.41
  76.4 2.4 %fusion.46 = bf16[32,4,64,8]{2,3,1,0:T(8,128)(2,1)} fusion(bf16[8,32,4,64]{3,2,1,0:T(4,128)(2,1)} %reshape.325, f32[32,4,8,8]{2,3,1,0:T(8,128)} %fusion.1), kind=kOutput, calls=%fused_computation.97 | convolution fusion | flops 1065991 | bytes 294912 | tf_op jit(solution)/shard_map/shlm,lshd->mshd/dot_general | solution.py:90
  78.8 1.1 copy.187
  79.9 2.1 %fusion.12 = (f32[8,32,4]{1,2,0:T(4,128)S(1)}, f32[8,32,4]{1,2,0:T(4,128)S(1)}) fusion(f32[32,4,64,8]{2,3,1,0:T(8,128)} %fusion.41, f32[8,32,3,4,64]{4,1,3,2,0:T(8,128)S(1)} %fusion.75, f32[8,32,4]{1,2,0:T(4,128)S(1)} %add_rsqrt_fusion.1, f32[8,32,4]{1,2,0:T(4,128)} %copy-done.22, f32[32,4,64,8]{2,3,1,0:T(8,128)} %fusion.49), kind=kLoop, calls=%fused_computation.41 | loop fusion | flops 522240 | bytes 1064960 | tf_op jit(solution)/shard_map/reduce_sum | solution.py:120
  83.4 1.3 copy.111
  84.7 1.9 reshape.326
  87.0 2.2 %all-gather.1 = bf16[512,512]{1,0:T(8,128)(2,1)S(1)} all-gather(bf16[256,512]{1,0:T(8,128)(2,1)S(1)} %convolution_convert_fusion.2), channel_id=3, replica_groups=mesh['grp'=2,'row'=8,'head'=2] {'head'}, dimensions={0}, use_global_device_ids=true | all-gather | bytes 786432 | tf_op jit(solution)/shard_map/all_gather | solution.py:152
  90.0 4.2 %all-to-all-start.2 = ((bf16[8,32,512]{2,1,0:T(8,128)(2,1)}), bf16[8,32,512]{2,1,0:T(8,128)(2,1)}, u32[]{:S(2)}, u32[]{:S(2)}) async-start(bf16[8,32,512]{2,1,0:T(8,128)(2,1)} %fusion.7), calls=%async_computation.2 | async-start | bytes 524288 | tf_op jit(solution)/shard_map/all_to_all | solution.py:180
  94.5 1.7 fusion.2
  96.2 1.1 copy.115
  98.6 1.1 convolution_bitcast_fusion.1
  99.6 1.5 fusion.28
  101.1 2.6 %all-to-all-done.2 = bf16[8,32,512]{2,1,0:T(8,128)(2,1)} async-done(((bf16[8,32,512]{2,1,0:T(8,128)(2,1)}), bf16[8,32,512]{2,1,0:T(8,128)(2,1)}, u32[]{:S(2)}, u32[]{:S(2)}) %all-to-all-start.2) | async-done | bytes 262176 | tf_op jit(solution)/shard_map/all_to_all | solution.py:180
  103.7 1.4 convolution_convert_fusion.5
  105.1 2.0 convolution_bitcast_fusion.2
  110.0 1.5 fusion.34
  111.5 1.9 copy.121
  113.4 3.5 %pad_maximum_fusion = f32[512,8,256]{2,0,1:T(8,128)} fusion(f32[512,1,256]{2,0,1:T(8,128)} %convolution_bitcast_fusion.1, f32[512,3,256]{2,0,1:T(8,128)S(1)} %fusion.28, f32[512,1,256]{2,0,1:T(8,128)} %convolution_bitcast_fusion.2, f32[512,3,256]{2,0,1:T(8,128)S(1)} %copy.121), kind=kLoop, calls=%fused_computation | loop fusion | flops 3145728 | bytes 8388608 | tf_op jit(solution)/shard_map/concatenate | solution.py:186
  116.9 1.1 copy-done.9
  118.5 2.2 %all-gather.2 = bf16[512,512]{1,0:T(8,128)(2,1)S(1)} all-gather(bf16[256,512]{1,0:T(8,128)(2,1)S(1)} %convolution_convert_fusion.1), channel_id=4, replica_groups=mesh['grp'=2,'row'=8,'head'=2] {'head'}, dimensions={0}, use_global_device_ids=true | all-gather | bytes 786432 | tf_op jit(solution)/shard_map/all_gather | solution.py:152
  120.8 1.7 fusion.6
  122.5 81.5 %reduce-scatter.2.cloned.1.call-done = f32[64,8,256]{2,0,1:T(8,128)} async-done(((f32[512,8,256]{2,0,1:T(8,128)}), f32[64,8,256]{2,0,1:T(8,128)}) %reduce-scatter.2.cloned.1.call-update) | async-done | bytes 524304 | tf_op jit(solution)/shard_map/reduce_scatter | solution.py:185
  204.0 1.1 broadcast_multiply_fusion
  205.1 1.1 copy.122
  (96 shorter events, 18.5 us)
Async XLA Ops:
  7.2 4.4 %copy-start.3 = (bf16[512,8,256]{2,1,0:T(8,128)(2,1)S(1)}, bf16[512,8,256]{2,1,0:T(8,128)(2,1)}, u32[]{:S(2)}) copy-start(bf16[512,8,256]{2,1,0:T(8,128)(2,1)} %param.4) | copy-start | bytes 6291460
  12.3 1.0 copy-start.10
  13.2 0.9 copy-start.8
  13.7 0.6 copy-start.24
  13.7 0.6 copy-start.26
  14.1 0.7 copy-start.18
  14.1 0.7 copy-start.20
  14.8 1.0 copy-start.15
  25.5 16.5 %all-to-all-start.1 = ((bf16[8,2,8192]{2,1,0:T(2,128)(2,1)}), bf16[8,2,8192]{2,1,0:T(2,128)(2,1)}, u32[]{:S(2)}, u32[]{:S(2)}) async-start(bf16[8,2,8192]{2,1,0:T(2,128)(2,1)} %reshape.350), calls=%async_computation.1 | async-start | bytes 524288 | tf_op jit(solution)/shard_map/all_to_all | solution.py:171
  42.0 13.2 %all-to-all-start = ((bf16[8,2,8192]{2,1,0:T(2,128)(2,1)}), bf16[8,2,8192]{2,1,0:T(2,128)(2,1)}, u32[]{:S(2)}, u32[]{:S(2)}) async-start(bf16[8,2,8192]{2,1,0:T(2,128)(2,1)} %reshape.348), calls=%async_computation | async-start | bytes 524288 | tf_op jit(solution)/shard_map/all_to_all | solution.py:172
  47.6 0.8 copy-start.1
  58.1 0.7 copy-start.6
  64.0 2.2 %copy-start.22 = (f32[8,32,4]{1,2,0:T(4,128)}, f32[8,32,4]{1,2,0:T(4,128)S(1)}, u32[]{:S(2)}) copy-start(f32[8,32,4]{1,2,0:T(4,128)S(1)} %add_rsqrt_fusion) | copy-start | bytes 12292
  66.6 0.7 copy-start.12
  66.6 0.8 copy-start.14
  71.8 3.4 %copy-start.13 = (bf16[8,32,4,64]{3,1,2,0:T(8,128)(2,1)S(1)}, bf16[8,32,4,64]{3,1,2,0:T(8,128)(2,1)}, u32[]{:S(2)}) copy-start(bf16[8,32,4,64]{3,1,2,0:T(8,128)(2,1)} %copy-done.12) | copy-start | bytes 393220
  78.8 3.3 %copy-start.4 = (f32[32,4,64,8]{2,3,1,0:T(8,128)S(1)}, f32[32,4,64,8]{2,3,1,0:T(8,128)}, u32[]{:S(2)}) copy-start(f32[32,4,64,8]{2,3,1,0:T(8,128)} %fusion.49) | copy-start | bytes 786436
  78.8 3.3 %copy-start.5 = (f32[32,4,64,8]{2,3,1,0:T(8,128)S(1)}, f32[32,4,64,8]{2,3,1,0:T(8,128)}, u32[]{:S(2)}) copy-start(f32[32,4,64,8]{2,3,1,0:T(8,128)} %fusion.41) | copy-start | bytes 786436
  78.8 3.3 %copy-start.23 = (f32[8,32,4]{1,2,0:T(4,128)S(1)}, f32[8,32,4]{1,2,0:T(4,128)}, u32[]{:S(2)}) copy-start(f32[8,32,4]{1,2,0:T(4,128)} %copy-done.22) | copy-start | bytes 12292
  83.4 3.2 %copy-start = (bf16[512,3,256]{0,2,1:T(8,128)(2,1)S(1)}, bf16[512,3,256]{0,2,1:T(8,128)(2,1)}, u32[]{:S(2)}) copy-start(bf16[512,3,256]{0,2,1:T(8,128)(2,1)} %copy.136) | copy-start | bytes 2359300
  86.6 2.7 %copy-start.7 = (bf16[1,256,512]{2,1,0:T(8,128)(2,1)S(1)}, bf16[1,256,512]{2,1,0:T(8,128)(2,1)}, u32[]{:S(2)}) copy-start(bf16[1,256,512]{2,1,0:T(8,128)(2,1)} %copy-done.6) | copy-start | bytes 786436
  90.0 6.2 %copy-start.2 = (bf16[256,1,512]{2,1,0:T(2,128)(2,1)S(1)}, bf16[256,1,512]{2,1,0:T(2,128)(2,1)}, u32[]{:S(2)}) copy-start(bf16[256,1,512]{2,1,0:T(2,128)(2,1)} %copy-done.1) | copy-start | bytes 786436
  90.0 13.7 %all-to-all-start.2 = ((bf16[8,32,512]{2,1,0:T(8,128)(2,1)}), bf16[8,32,512]{2,1,0:T(8,128)(2,1)}, u32[]{:S(2)}, u32[]{:S(2)}) async-start(bf16[8,32,512]{2,1,0:T(8,128)(2,1)} %fusion.7), calls=%async_computation.2 | async-start | bytes 524288 | tf_op jit(solution)/shard_map/all_to_all | solution.py:180
  94.2 109.8 %reduce-scatter.2.cloned.1.call-start = ((), (), s32[]{:S(2)}) async-start(), calls=%async_computation.4 | async-start | bytes 4718592 | tf_op jit(solution)/shard_map/reduce_scatter | solution.py:185
  107.8 0.9 copy-start.21
  107.8 1.2 copy-start.19
  107.8 1.2 copy-start.25
  107.8 1.2 copy-start.27
  109.0 1.0 copy-start.11
  109.4 2.0 copy-start.16
  116.9 1.1 copy-start.9
  116.9 1.2 copy-start.17
Sparse Core Ops, SparseCore 0:
  117.1 86.8 reduce-scatter.1
